TPU v7x, 512 devices: a whole 4x4x16 slice. The times are simulated.
512 devices in a mesh: seq: 64 (over z, y), head: 8 (over x, core).
Axes of the slice: x: 4, y: 4, z: 16, core: 2. Of those that a mesh axis runs over, the one named last changes fastest.
Arguments:
- inner_acts: bfloat16 [16384, 8192], P('seq', 'head'), may hold values from -0.4375 to 0.4375
- out_grad: bfloat16 [16384, 8192], P('seq', 'head'), may hold values from -0.4375 to 0.4375
- write_proj: bfloat16 [16384, 128], P('seq'), may hold values from -3 to 3
- read_proj: bfloat16 [16384, 128], P('seq'), may hold values from -3 to 3
- log_decay: float32 [16384, 64], P('seq', 'head'), may hold values from -2.5 to 0, as said below
- w_in: bfloat16 [4096, 8192], P('seq', 'head'), may hold values from -0.1875 to 0.1875
Outputs:
- input_grad: bfloat16 [16384, 4096], P('seq', 'head')
- act_grad: bfloat16 [16384, 8192], P('seq', 'head')
- write_grad: float32 [16384, 128], P('seq')
- read_grad: float32 [16384, 128], P('seq')
Inputs may be any that keep to these rules, and one draw needn't show every extreme that they name: `log_decay`: natural log of a decay factor of each head at each token; every entry is negative.
All inputs are finite; a program needn't handle non-finite values.
Results may differ from a plain program's by a relative error of at most 0.019.
Values may be sent and summed in bfloat16 or wider, within the bound.
A program may use at most 192 MiB of HBM per device.

v0:
```python
import jax
import jax.numpy as jnp
from jax import lax
from jax.sharding import PartitionSpec as P

SPAN = 256
exact_mode = lax.Precision.HIGHEST


def carried_in(shard, axis, combine, identity):
    devices, position = (lax.axis_size(axis), lax.axis_index(axis))
    everything = jax.tree.map(
        lambda part, kind: lax.all_gather(part.astype(kind), axis),
        shard,
        (jnp.bfloat16, jnp.bfloat16),
    )
    start = jax.tree.map(
        lambda part, zero: jnp.broadcast_to(jnp.asarray(zero, part.dtype), part.shape),
        shard,
        identity,
    )

    def step(k, before):
        reached = k < position
        new = combine(
            before, jax.tree.map(lambda part, own: part[k].astype(own.dtype), everything, shard)
        )
        return jax.tree.map(lambda a, b: jnp.where(reached, a, b), new, before)

    return lax.fori_loop(0, devices, step, start)


def carried_in_2(part, axis, combine, identity):
    count = lax.axis_size(axis)
    place = lax.axis_index(axis)
    ahead = count - 1 - place
    gathered = jax.tree.map(lambda a: lax.all_gather(a, axis), part)
    state = jax.tree.map(lambda a, e: jnp.zeros_like(a) + jnp.asarray(e, a.dtype), part, identity)

    def one(step, state):
        source = count - 1 - step
        return combine(
            state, jax.tree.map(lambda a: lax.dynamic_index_in_dim(a, source, 0, False), gathered)
        )

    return lax.fori_loop(0, ahead, one, state)


def decay_blocks(cumulative):
    count = cumulative.shape[1]
    by_head = jnp.swapaxes(cumulative, 1, 2)
    spread_log = by_head[:, :, :, None] - by_head[:, :, None, :]
    below_diag = jnp.arange(count)[:, None] >= jnp.arange(count)[None, :]
    return jnp.exp(jnp.where(below_diag, spread_log, -jnp.inf))


def combine(earlier, later):
    return (earlier[0] + later[0], jnp.exp(later[0])[:, None, None] * earlier[1] + later[1])


def local(inner_acts, out_grad, write_proj, read_proj, log_decay, w_in):
    tok_rows = inner_acts.shape[0]
    head_count = log_decay.shape[1]
    head_dim = inner_acts.shape[1] // head_count
    state_dim = write_proj.shape[1]
    blocks = tok_rows // SPAN
    act_narrow = inner_acts.reshape(blocks, SPAN, head_count, head_dim)
    grad_narrow = out_grad.reshape(blocks, SPAN, head_count, head_dim)
    act_blocks = act_narrow.astype(jnp.float32)
    grad_blocks = grad_narrow.astype(jnp.float32)
    write_blocks = write_proj.astype(jnp.float32).reshape(blocks, SPAN, state_dim)
    read_blocks = read_proj.astype(jnp.float32).reshape(blocks, SPAN, state_dim)
    cumulative = jnp.cumsum(log_decay.reshape(blocks, SPAN, head_count), axis=1)
    totals = cumulative[:, -1, :]
    tail_decay = jnp.exp(totals[:, None, :] - cumulative)
    head_decay = jnp.exp(cumulative)
    decays = decay_blocks(cumulative)
    weighted = decays * jnp.einsum(
        "kahp,kbhp->khab", grad_narrow, act_narrow, preferred_element_type=jnp.float32
    )
    read_local = jnp.einsum("khab,kbn->kan", weighted, write_blocks, precision=exact_mode)
    write_local = jnp.einsum("khab,kan->kbn", weighted, read_blocks, precision=exact_mode)
    scores = jnp.einsum(
        "kan,kbn->kab",
        read_proj.reshape(blocks, SPAN, state_dim),
        write_proj.reshape(blocks, SPAN, state_dim),
        preferred_element_type=jnp.float32,
    )
    act_local = jnp.einsum(
        "khab,kahp->kbhp", decays * scores[:, None], grad_blocks, precision=exact_mode
    )
    block_ends = jnp.einsum(
        "kbhp,kbn->khpn", act_blocks * tail_decay[..., None], write_blocks, precision=exact_mode
    )
    fronts = jnp.einsum(
        "kahp,kan->khpn", grad_blocks * head_decay[..., None], read_blocks, precision=exact_mode
    )
    zero_log = jnp.zeros((head_count,), jnp.float32)
    zero_state = jnp.zeros((head_count, head_dim, state_dim), jnp.float32)
    prefix_logs = []
    prefix_states = []
    running = (zero_log, zero_state)
    index = 0
    prefix_logs.append(running[0])
    prefix_states.append(running[1])
    running = combine(running, (totals[index], block_ends[index]))
    end_log, end_state = running
    suffix_logs = [zero_log] * blocks
    suffix_grads = [zero_state] * blocks
    running = (zero_log, zero_state)
    for index in reversed(range(blocks)):
        suffix_logs[index] = running[0]
        suffix_grads[index] = running[1]
        running = combine(running, (totals[index], fronts[index]))
    front_log, front_state = running
    state_in = carried_in((end_log, end_state), "seq", combine, (zero_log, zero_state))[1]
    grad_in = carried_in_2((front_log, front_state), "seq", combine, (zero_log, zero_state))[1]
    current = state_in
    index = 0
    states_list = [current]
    grads_list = [zero_state] * blocks
    current = grad_in
    for index in reversed(range(blocks)):
        grads_list[index] = current
        current = jnp.exp(totals[index])[:, None, None] * current + fronts[index]
    state_stack = jnp.stack(states_list)
    grad_stack = jnp.stack(grads_list)
    read_carry = jnp.einsum(
        "kahp,khpn->kan", grad_blocks * head_decay[..., None], state_stack, precision=exact_mode
    )
    write_carry = jnp.einsum(
        "kbhp,khpn->kbn", act_blocks * tail_decay[..., None], grad_stack, precision=exact_mode
    )
    act_carry = (
        jnp.einsum("khpn,kbn->kbhp", grad_stack, write_blocks, precision=exact_mode)
        * tail_decay[..., None]
    )
    act_grad = (act_local + act_carry).astype(jnp.bfloat16).reshape(tok_rows, head_count * head_dim)
    write_part = (write_local + write_carry).reshape(tok_rows, state_dim)
    read_part = (read_local + read_carry).reshape(tok_rows, state_dim)
    write_grad, read_grad = (
        lax.psum(write_part.astype(jnp.bfloat16), "head").astype(jnp.float32),
        lax.psum(read_part.astype(jnp.bfloat16), "head").astype(jnp.float32),
    )
    group_term = lax.dot_general(
        act_grad,
        lax.all_gather(w_in, "seq", axis=0, tiled=True),
        (((1,), (1,)), ((), ())),
        preferred_element_type=jnp.float32,
    )
    input_grad = lax.psum_scatter(
        group_term.astype(jnp.bfloat16).astype(jnp.float32).astype(jnp.bfloat16),
        "head",
        scatter_dimension=1,
        tiled=True,
    )
    return (input_grad, act_grad, write_grad, read_grad)


def solution(mesh):
    return jax.shard_map(
        local,
        mesh=mesh,
        in_specs=(
            P("seq", "head"),
            P("seq", "head"),
            P("seq", None),
            P("seq", None),
            P("seq", "head"),
            P("seq", "head"),
        ),
        out_specs=(P("seq", "head"), P("seq", "head"), P("seq", None), P("seq", None)),
        check_vma=False,
    )
```

profile of v0, /device:TPU:8, one launch (start us, length us, event | category | flops | bytes accessed | tf_op | source)
XLA Modules:
  0.0 784.8 jit_solution(3327351343411042735)
XLA Ops:
  7.2 1.3 reduce-window.6
  11.4 1.3 fusion.14
  13.1 1.8 convolution_add_fusion.1
  17.9 85.3 %all-gather = f32[64,1,8]{2,1,0:T(1,128)} all-gather(f32[1,1,8]{2,1,0:T(1,128)S(1)} %copy-done.7), channel_id=2, replica_groups=mesh['seq'=64,'head'=8] {'seq'}, dimensions={0}, use_global_device_ids=true | all-gather | bytes 2080 | tf_op jit(solution)/shard_map/all_gather | solution.py:37
  104.5 73.1 %all-gather.3 = bf16[64,1,8]{2,1,0:T(2,128)(2,1)S(1)} all-gather(bf16[1,1,8]{2,1,0:T(2,128)(2,1)} %slice.19), channel_id=5, replica_groups=mesh['seq'=64,'head'=8] {'seq'}, dimensions={0}, use_global_device_ids=true | all-gather | bytes 1040 | tf_op jit(solution)/shard_map/all_gather | solution.py:13
  178.2 1.7 multiply_reduce_fusion
  179.9 30.1 %all-gather.12.cloned.1.call-done = bf16[512,128,128]{2,1,0:T(8,128)(2,1)} async-done(((bf16[8,128,128]{2,1,0:T(8,128)(2,1)}), bf16[512,128,128]{2,1,0:T(8,128)(2,1)}) %all-gather.12.cloned.1.call-update) | async-done | bytes 16777232 | tf_op jit(solution)/shard_map/all_gather | solution.py:13
  210.0 115.6 %while.29 = (s32[]{:T(128)}, f32[8,128,128]{2,1,0:T(8,128)S(1)}, s32[]{:T(128)}, bf16[64,8]{1,0:T(8,128)(2,1)}, bf16[64,8,128,128]{3,2,1,0:T(8,128)(2,1)}, /*index=5*/s32[]{:T(128)}, s32[]{:T(128)}) while((s32[]{:T(128)}, f32[8,128,128]{2,1,0:T(8,128)S(1)}, s32[]{:T(128)}, bf16[64,8]{1,0:T(8,128)(2,1)}, ...), condition=%wide.region_8.9_spmd.clone, body=%wide.region_7.8_spmd.clone.sunk | while | flops 655372 | bytes 1310905 | solution.py:30
  327.6 176.6 %all-gather.10.cloned.1.call-done = f32[512,128,128]{2,1,0:T(8,128)} async-done(((f32[8,128,128]{2,1,0:T(8,128)}), f32[512,128,128]{2,1,0:T(8,128)}) %all-gather.10.cloned.1.call-update) | async-done | bytes 33554448 | tf_op jit(solution)/shard_map/all_gather | solution.py:37
  504.3 118.4 %while.28 = (s32[]{:T(128)}, f32[8,128,128]{2,1,0:T(8,128)S(1)}, s32[]{:T(128)}, f32[64,8]{1,0:T(8,128)}, f32[64,8,128,128]{3,2,1,0:T(8,128)}, /*index=5*/s32[]{:T(128)}, s32[]{:T(128)}, s32[]{:T(128)}, s32[]{:T(128)}) while((s32[]{:T(128)}, f32[8,128,128]{2,1,0:T(8,128)S(1)}, s32[]{:T(128)}, f32[64,8]{1,0:T(8,128)}, ...), condition=%wide.region_3.4_spmd, body=%wide.region_2.3_spmd.sunk | while | flops 262150 | bytes 1573107 | solution.py:46
  505.0 1.2 bitcast_add_fusion.5
  506.9 1.2 bitcast_add_fusion.5
  512.6 1.2 bitcast_add_fusion.5
  520.3 1.2 bitcast_add_fusion.5
  524.1 1.2 bitcast_add_fusion.5
  529.8 1.2 bitcast_add_fusion.5
  545.0 1.2 bitcast_add_fusion.5
  550.8 1.2 bitcast_add_fusion.5
  552.7 1.2 bitcast_add_fusion.5
  556.5 1.2 bitcast_add_fusion.5
  558.4 1.2 bitcast_add_fusion.5
  560.3 1.2 bitcast_add_fusion.5
  564.1 1.2 bitcast_add_fusion.5
  566.0 1.2 bitcast_add_fusion.5
  567.9 1.2 bitcast_add_fusion.5
  569.8 1.2 bitcast_add_fusion.5
  573.6 1.2 bitcast_add_fusion.5
  575.5 1.2 bitcast_add_fusion.5
  577.4 1.2 bitcast_add_fusion.5
  579.3 1.2 bitcast_add_fusion.5
  583.1 1.2 bitcast_add_fusion.5
  588.8 1.2 bitcast_add_fusion.5
  590.7 1.3 bitcast_add_fusion.5
  600.4 1.2 bitcast_add_fusion.5
  602.3 1.2 bitcast_add_fusion.5
  606.1 1.2 bitcast_add_fusion.5
  611.9 1.2 bitcast_add_fusion.5
  615.7 1.2 bitcast_add_fusion.5
  619.5 1.2 bitcast_add_fusion.5
  621.4 1.2 bitcast_add_fusion.5
  623.3 1.8 convolution_bitcast_fusion.2
  626.1 2.4 fusion.11
  628.8 31.9 %all-gather.8.cloned.1.call-done = bf16[4096,1024]{1,0:T(8,128)(2,1)} async-done(((bf16[64,1024]{1,0:T(8,128)(2,1)}), bf16[4096,1024]{1,0:T(8,128)(2,1)}) %all-gather.8.cloned.1.call-update) | async-done | bytes 8388624 | tf_op jit(solution)/shard_map/all_gather | solution.py:147
  660.7 7.1 convolution_convert_fusion
  668.8 65.5 %all-reduce.3.cloned.1.call-done = (bf16[256,128]{1,0:T(8,128)(2,1)}, bf16[256,128]{1,0:T(8,128)(2,1)}) async-done(((bf16[256,128]{1,0:T(8,128)(2,1)}, bf16[256,128]{1,0:T(8,128)(2,1)}), (bf16[256,128]{1,0:T(8,128)(2,1)}, bf16[256,128]{1,0:T(8,128)(2,1)})) %all-reduce.3.cloned.1.call-update) | async-done | bytes 131088 | tf_op jit(solution)/shard_map/psum | solution.py:142
  734.3 1.5 convert_element_type.84
  735.8 1.5 convert_element_type.89
  737.3 40.9 %reduce-scatter.2.cloned.1.call-done = bf16[256,512]{1,0:T(8,128)(2,1)} async-done(((bf16[256,4096]{1,0:T(8,128)(2,1)}), bf16[256,512]{1,0:T(8,128)(2,1)}) %reduce-scatter.2.cloned.1.call-update) | async-done | bytes 262160 | tf_op jit(solution)/shard_map/reduce_scatter | solution.py:151
  (276 shorter events, 208.1 us)
Async XLA Ops:
  7.2 3.9 copy-start
  7.2 3.3 copy-start.3
  7.2 202.8 %all-gather.12.cloned.1.call-start = ((), (), s32[]{:S(2)}) async-start(), calls=%async_computation.4 | async-start | bytes 17039360 | tf_op jit(solution)/shard_map/all_gather | solution.py:13
  8.8 1.8 copy-start.4
  10.7 0.7 copy-start.6
  10.7 2.4 copy-start.1
  10.7 2.4 copy-start.2
  12.7 491.5 %all-gather.10.cloned.1.call-start = ((), (), s32[]{:S(2)}) async-start(), calls=%async_computation.3 | async-start | bytes 34078720 | tf_op jit(solution)/shard_map/all_gather | solution.py:37
  13.1 4.8 copy-start.7
  15.0 645.7 %all-gather.8.cloned.1.call-start = ((), (), s32[]{:S(2)}) async-start(), calls=%async_computation.1 | async-start | bytes 8519680 | tf_op jit(solution)/shard_map/all_gather | solution.py:147
  15.7 718.6 %all-reduce.3.cloned.1.call-start = ((), (), s32[]{:S(2)}) async-start(), calls=%async_computation.5 | async-start | bytes 262144 | tf_op jit(solution)/shard_map/psum | solution.py:142
  622.7 3.4 copy-start.5
  628.6 149.7 %reduce-scatter.2.cloned.1.call-start = ((), (), s32[]{:S(2)}) async-start(), calls=%async_computation.2 | async-start | bytes 2359296 | tf_op jit(solution)/shard_map/reduce_scatter | solution.py:151
Sparse Core Ops, SparseCore 0:
  12.8 197.1 all-gather.11
  213.5 290.6 all-gather.9
  507.2 153.4 all-gather.7
  663.5 70.7 all-reduce.2
  737.8 40.4 reduce-scatter.1
where the time goes:
time: 794 us; the launch traced here: 785 us
  waiting for transfers between devices  346 us (44%)
  other arithmetic  195 us (25%)
  blocking collectives  158 us (20%)
  local copies, waits for them, and re-layouts  48 us (6%)
  matrix products  20.7 us (3%)
  between operations  14 us (2%)
    all_gather x1, waiting for transfers between devices, carried_in_2(): gathered = jax.tree.map(lambda a: lax.all_gather(a, axis), part)  177 us
    all_gather x1, blocking collectives, carried_in_2(): gathered = jax.tree.map(lambda a: lax.all_gather(a, axis), part)  85.3 us
    add x62, other arithmetic, combine(): jnp.exp(later[0])[:, None, None] * earlier[1] + later[1]  73.9 us
    all_gather x1, blocking collectives, carried_in(): lax.all_gather(part.astype(kind), axis)  73.1 us
    select_n x64, other arithmetic, step(): return jax.tree.map(lambda a, b: jnp.where(reached, a, b), new, before)  70.1 us
    psum x1, waiting for transfers between devices, local(): lax.psum(write_part.astype(jnp.bfloat16), 'head').astype(jnp.float32)  65.5 us
    exp x64, other arithmetic, combine(): jnp.exp(later[0])[:, None, None] * earlier[1] + later[1]  44.4 us
    exp x62, local copies, waits for them, and re-layouts, combine(): jnp.exp(later[0])[:, None, None] * earlier[1] + later[1]  42.7 us
  transfers between devices with their start and end apart: 5, of which 5 were waited for; matrix products, arithmetic and copies ran while one was open for 33% of the time, Pallas kernels for 0%

commit v1 on v0

--- a/solution.py
+++ b/solution.py
@@ -144,7 +144,9 @@
     )
     group_term = lax.dot_general(
         act_grad,
-        lax.all_gather(w_in, "seq", axis=0, tiled=True),
+        jnp.concatenate(
+            lax.all_to_all(jnp.stack([w_in] * lax.axis_size("seq")), "seq", 0, 0), axis=0
+        ),
         (((1,), (1,)), ((), ())),
         preferred_element_type=jnp.float32,
     )

time: 794 us -> 1050 us (1.32)
  blocking collectives: 158 us -> 583 us
  waiting for transfers between devices: 346 us -> 154 us
  starting transfers between devices: 0.38 us -> 19.3 us
    all_gather x1, blocking collectives: 73.1 us -> 506 us  [carried_in(): lax.all_gather(part.astype(kind), axis)]
    all_gather x1, waiting for transfers between devices: 177 us -> 56.8 us  [carried_in_2(): gathered = jax.tree.map(lambda a: lax.all_gather(a, axis), part)]
    all_gather x1 -> x0, waiting for transfers between devices: 31.9 us -> none  [local(): lax.all_gather(w_in, 'seq', axis=0, tiled=True)]
    all_gather x1, waiting for transfers between devices: 30.1 us -> 0.02 us  [carried_in(): lax.all_gather(part.astype(kind), axis)]
    all_to_all x0 -> x1, starting transfers between devices: none -> 18.9 us  [local(): lax.all_to_all(jnp.stack([w_in] * lax.axis_size('seq')), 'seq', 0, 0)]
  transfers between devices with their start and end apart: 5 -> 5, of which waited for: 5 -> 3; matrix products, arithmetic and copies ran while one was open for 33% -> 25% of each run, Pallas kernels for 0% -> 0%
where the time goes in v1:
time: 1050 us; the launch traced here: 1040 us
  blocking collectives  583 us (56%)
  other arithmetic  193 us (18%)
  waiting for transfers between devices  154 us (15%)
  local copies, waits for them, and re-layouts  52.1 us (5%)
  matrix products  19.8 us (2%)
  starting transfers between devices  19.3 us (2%)
  between operations  14.1 us (1%)
    all_gather x1, blocking collectives, carried_in(): lax.all_gather(part.astype(kind), axis)  506 us
    all_gather x1, blocking collectives, carried_in_2(): gathered = jax.tree.map(lambda a: lax.all_gather(a, axis), part)  76.8 us
    add x62, other arithmetic, combine(): jnp.exp(later[0])[:, None, None] * earlier[1] + later[1]  73.6 us
    select_n x64, other arithmetic, step(): return jax.tree.map(lambda a, b: jnp.where(reached, a, b), new, before)  70.2 us
    all_gather x1, waiting for transfers between devices, carried_in_2(): gathered = jax.tree.map(lambda a: lax.all_gather(a, axis), part)  56.8 us
    psum x1, waiting for transfers between devices, local(): lax.psum(write_part.astype(jnp.bfloat16), 'head').astype(jnp.float32)  56.1 us
    exp x64, other arithmetic, combine(): jnp.exp(later[0])[:, None, None] * earlier[1] + later[1]  44.4 us
    exp x62, local copies, waits for them, and re-layouts, combine(): jnp.exp(later[0])[:, None, None] * earlier[1] + later[1]  42.6 us
  transfers between devices with their start and end apart: 5, of which 3 were waited for; matrix products, arithmetic and copies ran while one was open for 25% of the time, Pallas kernels for 0%

profile of v1, /device:TPU:8, one launch (start us, length us, event | category | flops | bytes accessed | tf_op | source)
XLA Modules:
  0.0 1038.5 jit_solution(15842452310401971215)
XLA Ops:
  7.2 1.3 reduce-window.6
  11.3 1.3 fusion.14
  13.0 1.8 convolution_add_fusion.1
  14.9 4.3 stack.2
  19.2 18.9 %all-to-all-start = ((bf16[64,64,1024]{2,1,0:T(8,128)(2,1)}), bf16[64,64,1024]{2,1,0:T(8,128)(2,1)}, u32[]{:S(2)}, u32[]{:S(2)}) async-start(bf16[64,64,1024]{2,1,0:T(8,128)(2,1)} %stack.2), calls=%async_computation | async-start | bytes 16777216 | tf_op jit(solution)/shard_map/all_to_all | solution.py:148
  39.4 506.3 %all-gather.3 = bf16[64,1,8]{2,1,0:T(2,128)(2,1)S(1)} all-gather(bf16[1,1,8]{2,1,0:T(2,128)(2,1)} %slice.19), channel_id=5, replica_groups=mesh['seq'=64,'head'=8] {'seq'}, dimensions={0}, use_global_device_ids=true | all-gather | bytes 1040 | tf_op jit(solution)/shard_map/all_gather | solution.py:13
  546.3 76.8 %all-gather = f32[64,1,8]{2,1,0:T(1,128)} all-gather(f32[1,1,8]{2,1,0:T(1,128)} %get-tuple-element.277), channel_id=2, replica_groups=mesh['seq'=64,'head'=8] {'seq'}, dimensions={0}, use_global_device_ids=true | all-gather | bytes 2080 | tf_op jit(solution)/shard_map/all_gather | solution.py:37
  624.1 1.7 multiply_reduce_fusion
  625.8 115.7 %while.29 = (s32[]{:T(128)}, f32[8,128,128]{2,1,0:T(8,128)S(1)}, s32[]{:T(128)}, bf16[64,8]{1,0:T(8,128)(2,1)}, bf16[64,8,128,128]{3,2,1,0:T(8,128)(2,1)}, /*index=5*/s32[]{:T(128)}, s32[]{:T(128)}) while((s32[]{:T(128)}, f32[8,128,128]{2,1,0:T(8,128)S(1)}, s32[]{:T(128)}, bf16[64,8]{1,0:T(8,128)(2,1)}, ...), condition=%wide.region_8.9_spmd.clone, body=%wide.region_7.8_spmd.clone.sunk | while | flops 655372 | bytes 1310905 | solution.py:30
  743.5 56.8 %all-gather.7.cloned.1.call-done = f32[512,128,128]{2,1,0:T(8,128)} async-done(((f32[8,128,128]{2,1,0:T(8,128)}), f32[512,128,128]{2,1,0:T(8,128)}) %all-gather.7.cloned.1.call-update) | async-done | bytes 33554448 | tf_op jit(solution)/shard_map/all_gather | solution.py:37
  800.4 118.0 %while.28 = (s32[]{:T(128)}, f32[8,128,128]{2,1,0:T(8,128)S(1)}, s32[]{:T(128)}, f32[64,8]{1,0:T(8,128)}, f32[64,8,128,128]{3,2,1,0:T(8,128)}, /*index=5*/s32[]{:T(128)}, s32[]{:T(128)}, s32[]{:T(128)}, s32[]{:T(128)}) while((s32[]{:T(128)}, f32[8,128,128]{2,1,0:T(8,128)S(1)}, s32[]{:T(128)}, f32[64,8]{1,0:T(8,128)}, ...), condition=%wide.region_3.4_spmd, body=%wide.region_2.3_spmd.sunk | while | flops 262150 | bytes 1573107 | solution.py:46
  801.1 1.2 bitcast_add_fusion.5
  803.1 1.2 bitcast_add_fusion.5
  805.0 1.2 bitcast_add_fusion.5
  806.9 1.2 bitcast_add_fusion.5
  808.8 1.2 bitcast_add_fusion.5
  810.7 1.2 bitcast_add_fusion.5
  812.6 1.2 bitcast_add_fusion.5
  814.5 1.2 bitcast_add_fusion.5
  818.3 1.2 bitcast_add_fusion.5
  822.1 1.2 bitcast_add_fusion.5
  827.8 1.2 bitcast_add_fusion.5
  833.5 1.2 bitcast_add_fusion.5
  835.5 1.2 bitcast_add_fusion.5
  841.2 1.2 bitcast_add_fusion.5
  864.0 1.2 bitcast_add_fusion.5
  869.6 1.2 bitcast_add_fusion.5
  871.5 1.2 bitcast_add_fusion.5
  879.1 1.2 bitcast_add_fusion.5
  884.9 1.2 bitcast_add_fusion.5
  890.6 1.2 bitcast_add_fusion.5
  894.4 1.2 bitcast_add_fusion.5
  896.3 1.2 bitcast_add_fusion.5
  900.1 1.2 bitcast_add_fusion.5
  905.8 1.2 bitcast_add_fusion.5
  907.7 1.2 bitcast_add_fusion.5
  909.6 1.2 bitcast_add_fusion.5
  911.5 1.2 bitcast_add_fusion.5
  913.4 1.2 bitcast_add_fusion.5
  915.4 1.2 bitcast_add_fusion.5
  917.3 1.2 bitcast_add_fusion.5
  918.5 1.8 convolution_bitcast_fusion.2
  922.2 1.5 fusion.11
  923.7 7.1 convolution_convert_fusion
  931.9 56.1 %all-reduce.3.cloned.1.call-done = (bf16[256,128]{1,0:T(8,128)(2,1)}, bf16[256,128]{1,0:T(8,128)(2,1)}) async-done(((bf16[256,128]{1,0:T(8,128)(2,1)}, bf16[256,128]{1,0:T(8,128)(2,1)}), (bf16[256,128]{1,0:T(8,128)(2,1)}, bf16[256,128]{1,0:T(8,128)(2,1)})) %all-reduce.3.cloned.1.call-update) | async-done | bytes 131088 | tf_op jit(solution)/shard_map/psum | solution.py:142
  988.0 1.5 convert_element_type.84
  989.5 1.5 convert_element_type.89
  991.0 40.9 %reduce-scatter.2.cloned.1.call-done = bf16[256,512]{1,0:T(8,128)(2,1)} async-done(((bf16[256,4096]{1,0:T(8,128)(2,1)}), bf16[256,512]{1,0:T(8,128)(2,1)}) %reduce-scatter.2.cloned.1.call-update) | async-done | bytes 262160 | tf_op jit(solution)/shard_map/reduce_scatter | solution.py:153
  (284 shorter events, 206.0 us)
Async XLA Ops:
  7.2 3.9 copy-start
  7.2 3.3 copy-start.3
  7.2 618.6 %all-gather.9.cloned.1.call-start = ((), (), s32[]{:S(2)}) async-start(), calls=%async_computation.4 | async-start | bytes 17039360 | tf_op jit(solution)/shard_map/all_gather | solution.py:13
  8.8 1.7 copy-start.8
  10.6 0.7 copy-start.11
  10.7 2.4 copy-start.1
  10.7 2.4 copy-start.2
  12.6 2.3 copy-start.5
  12.6 787.7 %all-gather.7.cloned.1.call-start = ((), (), s32[]{:S(2)}) async-start(), calls=%async_computation.3 | async-start | bytes 34078720 | tf_op jit(solution)/shard_map/all_gather | solution.py:37
  19.2 904.5 %all-to-all-start = ((bf16[64,64,1024]{2,1,0:T(8,128)(2,1)}), bf16[64,64,1024]{2,1,0:T(8,128)(2,1)}, u32[]{:S(2)}, u32[]{:S(2)}) async-start(bf16[64,64,1024]{2,1,0:T(8,128)(2,1)} %stack.2), calls=%async_computation | async-start | bytes 16777216 | tf_op jit(solution)/shard_map/all_to_all | solution.py:148
  38.1 949.9 %all-reduce.3.cloned.1.call-start = ((), (), s32[]{:S(2)}) async-start(), calls=%async_computation.5 | async-start | bytes 262144 | tf_op jit(solution)/shard_map/psum | solution.py:142
  623.1 0.9 copy-start.6
  623.2 0.9 copy-start.9
  918.5 3.7 copy-start.4
  918.5 3.7 copy-start.7
  918.5 3.7 copy-start.10
  921.4 110.6 %reduce-scatter.2.cloned.1.call-start = ((), (), s32[]{:S(2)}) async-start(), calls=%async_computation.2 | async-start | bytes 2359296 | tf_op jit(solution)/shard_map/reduce_scatter | solution.py:153
Sparse Core Ops, SparseCore 0:
  12.8 492.8 all-gather.8
  509.2 291.1 all-gather.6
  921.5 66.5 all-reduce.2
  991.5 40.4 reduce-scatter.1
